TPU v7x, 256 devices: a whole 4x4x8 slice. The times are simulated.
256 devices in a mesh: seq: 128 (over x, y, z), tp: 2 (over core).
Axes of the slice: x: 4, y: 4, z: 8, core: 2. Of those that a mesh axis runs over, the one named last changes fastest.
Arguments:
- hidden_acts: bfloat16 [32768, 28672], P('seq', 'tp'), may hold values from -6 to 6
- out_grads: bfloat16 [32768, 8192], P('seq', 'tp'), may hold values from -6 to 6
- proj_in: bfloat16 [28672, 64], P('tp'), may hold values from -0.03125 to 0.03125
- proj_out: bfloat16 [8192, 64], P('tp'), may hold values from -0.0625 to 0.0625
- doc_lengths: int32 [128], replicated, may hold values from 1 to 1024, 32768 in all
- owner: int32 [128], replicated, may hold values from 0 to 127, each once
- queries: float32 [4096, 4096], P(('seq', 'tp')), may hold values from -0.1 to 0.1
Outputs:
- store: float32 [128, 4096], P('seq')
- scores: float32 [4096, 128], P(('seq', 'tp'))
Inputs may be any that keep to these rules, and one draw needn't show every extreme that they name: Every document has its own owner. `doc_lengths`: the lengths sum to 32768.
All inputs are finite; a program needn't handle non-finite values.
Results may differ from a plain program's by a relative error of at most 0.0003.
Values sent between devices are 32-bit elements; how exact they have to be, the bound alone decides.
A program may use at most 64 MiB of HBM per device.

v0:
```python
import jax
import jax.numpy as jnp
from jax import lax
from jax.sharding import PartitionSpec as P


def normalize(table):
    return table / jnp.sqrt(jnp.mean(table * table, axis=1, keepdims=True) + 1e-06)


def per_device(hidden_acts, out_grads, proj_in, proj_out, doc_lengths, owner, queries):
    rank = proj_in.shape[1]
    left_part = jnp.dot(hidden_acts, proj_in, preferred_element_type=jnp.float32)
    right_part = jnp.dot(out_grads, proj_out, preferred_element_type=jnp.float32)
    stacked = jnp.concatenate([left_part, right_part], axis=1)
    halves = lax.psum_scatter(stacked, "tp", scatter_dimension=0, tiled=True)
    count = halves.shape[0]
    ends = jnp.cumsum(doc_lengths)
    starts = ends - doc_lengths
    base = lax.axis_index("seq") * hidden_acts.shape[0] + lax.axis_index("tp") * count
    positions = base + jnp.arange(count)
    member = (
        (starts[:, None] <= positions[None, :]) & (positions[None, :] < ends[:, None])
    ).astype(jnp.float32)
    outer = (halves[:, :rank, None] * halves[:, None, rank:]).reshape(count, rank * rank)
    partial_table = jnp.dot(member, outer, precision=lax.Precision.HIGHEST)
    grads = lax.psum(partial_table, ("seq", "tp"))
    normed = normalize(grads)
    mine = (owner == lax.axis_index("seq")).astype(jnp.float32)[None, :]
    store_row = jnp.dot(mine, normed, precision=lax.Precision.HIGHEST)
    scores = jnp.dot(queries, normed.T, precision=lax.Precision.HIGHEST)
    return (store_row, scores)


def solution(mesh):
    in_specs = (
        P("seq", "tp"),
        P("seq", "tp"),
        P("tp", None),
        P("tp", None),
        P(),
        P(),
        P(("seq", "tp"), None),
    )
    out_specs = (P("seq", None), P(("seq", "tp"), None))
    return jax.shard_map(
        per_device, mesh=mesh, in_specs=in_specs, out_specs=out_specs, check_vma=False
    )
```

profile of v0, /device:TPU:1, one launch (start us, length us, event | category | flops | bytes accessed | tf_op | source)
XLA Modules:
  0.0 310.9 jit_solution(10741195937966987048)
XLA Ops:
  7.2 0.0 copy-start
  7.2 0.0 copy-start.2
  7.2 0.0 reduce-scatter.2.cloned.1.call-start
  7.2 6.1 %fusion.12 = f32[256,64]{0,1:T(8,128)S(1)} fusion(bf16[256,14336]{1,0:T(8,128)(2,1)} %param.7, bf16[14336,64]{0,1:T(8,128)(2,1)} %param.9), kind=kOutput, calls=%fused_computation.19 | convolution fusion | flops 469762048 | bytes 9240576 | tf_op jit(solution)/shard_map/dot_general | solution.py:13
  13.3 0.0 copy-done
  13.3 0.0 copy-done.2
  13.3 0.0 copy-start.3
  13.3 0.8 fusion.13
  14.1 0.7 pad_maximum_fusion
  14.8 0.0 reduce-scatter.2.cloned.1.call-update
  14.8 0.0 all-reduce.2.cloned.1.call-start
  14.8 0.0 copy-done.3
  14.8 0.1 copy.12
  15.0 0.2 reduce-window.8
  15.1 0.1 reduce
  15.3 17.0 %reduce-scatter.2.cloned.1.call-done = f32[128,128]{0,1:T(8,128)} async-done(((f32[256,128]{0,1:T(8,128)}), f32[128,128]{0,1:T(8,128)}) %reduce-scatter.2.cloned.1.call-update) | async-done | bytes 65552 | tf_op jit(solution)/shard_map/reduce_scatter | solution.py:16
  32.3 0.8 fusion.11
  33.1 0.3 broadcast_multiply_fusion
  33.3 2.6 fusion.1
  35.9 0.0 copy-start.4
  35.9 0.0 all-reduce.2.cloned.1.call-update
  35.9 262.0 %all-reduce.2.cloned.1.call-done = f32[128,4096]{1,0:T(8,128)} async-done(((f32[128,4096]{1,0:T(8,128)}), f32[128,4096]{1,0:T(8,128)}) %all-reduce.2.cloned.1.call-update) | async-done | bytes 2097168 | tf_op jit(solution)/shard_map/psum | solution.py:27
  297.9 0.0 copy-start.1
  297.9 2.0 multiply_reduce_fusion
  299.9 0.0 copy-done.4
  299.9 0.2 copy-done.1
  300.1 0.0 copy-start.5
  300.1 2.4 convolution_bitcast_fusion
  302.6 0.0 copy-done.5
  302.6 1.5 fusion
  (3 shorter events, 0.0 us)
Async XLA Ops:
  7.2 6.2 %copy-start = (bf16[256,4096]{1,0:T(8,128)(2,1)S(1)}, bf16[256,4096]{1,0:T(8,128)(2,1)}, u32[]{:S(2)}) copy-start(bf16[256,4096]{1,0:T(8,128)(2,1)} %param.8) | copy-start | bytes 6291460
  7.2 6.1 %copy-start.2 = (bf16[4096,64]{0,1:T(8,128)(2,1)S(1)}, bf16[4096,64]{0,1:T(8,128)(2,1)}, u32[]{:S(2)}) copy-start(bf16[4096,64]{0,1:T(8,128)(2,1)} %param.10) | copy-start | bytes 1572868
  7.2 25.1 %reduce-scatter.2.cloned.1.call-start = ((), (), s32[]{:S(2)}) async-start(), calls=%async_computation.1 | async-start | bytes 196608 | tf_op jit(solution)/shard_map/reduce_scatter | solution.py:16
  13.3 1.5 copy-start.3
  14.8 283.1 %all-reduce.2.cloned.1.call-start = ((), (), s32[]{:S(2)}) async-start(), calls=%async_computation.2 | async-start | bytes 4194304 | tf_op jit(solution)/shard_map/psum | solution.py:27
  35.9 264.0 %copy-start.4 = (f32[16,4096]{1,0:T(8,128)S(1)}, f32[16,4096]{1,0:T(8,128)}, u32[]{:S(2)}) copy-start(f32[16,4096]{1,0:T(8,128)} %param.13) | copy-start | bytes 786436
  297.9 2.2 copy-start.1
  300.1 2.4 copy-start.5
Sparse Core Ops, SparseCore 0:
  14.9 17.3 reduce-scatter.1
  37.7 260.1 all-reduce.1
where the time goes:
time: 312 us; the launch traced here: 311 us
  waiting for transfers between devices  279 us (89%)
  between operations  14.1 us (5%)
  matrix products  13.3 us (4%)
  other arithmetic  3.17 us (1%)
    psum x1, waiting for transfers between devices, per_device(): grads = lax.psum(partial_table, ('seq', 'tp'))  262 us
    reduce_scatter x1, waiting for transfers between devices, per_device(): halves = lax.psum_scatter(stacked, 'tp', scatter_dimension=0, tiled=True)  17 us
  transfers between devices with their start and end apart: 2, of which 2 were waited for; matrix products, arithmetic and copies ran while one was open for 0% of the time, Pallas kernels for 0%

commit v1 on v0

v1 whole, which is shorter than its diff:
```python
import jax
import jax.numpy as jnp
from jax import lax
from jax.experimental import pallas as pl
from jax.experimental.pallas import tpu as pltpu
from jax.sharding import PartitionSpec as P

X, Y, Z = 4, 4, 8
RANK = 64
TOK = 256
HALF = 128
DOCS = 128
COLS = RANK * RANK
PLANE = X * Y * 2
MESH = pl.DeviceIdType.MESH
NT = (((1,), (1,)), ((), ()))
F32, BF16 = jnp.float32, jnp.bfloat16
PARTS = ((20, 20, 16), (20, 20, 12, 4))


def ring(step, size):
    return min(step, size - step)


FAR = sorted(
    [(a, b, c) for a in range(X) for b in range(Y) for c in range(2) if (a, b, c) != (0, 0, 0)],
    key=lambda o: -(ring(o[0], X) + ring(o[1], Y)),
)
FAR_Z = sorted(range(1, Z), key=lambda d: -ring(d, Z))


def split(v):
    hi = v.astype(BF16)
    return hi, (v - hi.astype(F32)).astype(BF16)


def dot(a, b):
    return jnp.dot(a, b, preferred_element_type=F32)


def kernel(
    hid, og, pin, pout, lens, owner, queries, store, scores,
    hid_v, og_v, pin_v, pout_v, q_v, acc, sib_out, sib_in, right, left, xr, xl,
    member, outer, qs, qr, qcat, part, rs, mine, ag, fs, fr,
    load_sem, sib_send, sib_recv, x_send, x_recv, z_send, z_recv,
):
    s, c = lax.axis_index("seq"), lax.axis_index("tp")
    x, y, z = s // (Y * Z), (s // Z) % Y, s % Z
    me = (x * Y + y) * 2 + c
    live = s >= 0

    def peer(o):
        x2, y2, c2 = (x + o[0]) % X, (y + o[1]) % Y, (c + o[2]) % 2
        return x2, y2, c2, (x2 * Y + y2) * 2 + c2, ((x2 * Y + y2) * Z + z, c2)

    def along_z(d):
        z2 = (z + d) % Z
        return z2, ((x * Y + y) * Z + z2, c)

    def remote(src, dst, send, recv, device):
        return pltpu.make_async_remote_copy(
            src_ref=src, dst_ref=dst, send_sem=send, recv_sem=recv, device_id=device, device_id_type=MESH
        )

    def settle(ref, sem):
        pltpu.make_async_copy(ref, ref, sem).wait()

    started = []

    def load(src, dst):
        copy = pltpu.make_async_copy(src, dst, load_sem.at[len(started)])
        copy.start()
        started.append(copy)
        return copy

    rows = [pl.ds(pl.multiple_of((1 - c) * HALF, HALF), HALF), pl.ds(pl.multiple_of(c * HALF, HALF), HALF)]
    at = [pl.ds(0, HALF), pl.ds(HALF, HALF)]
    jobs = []
    for h in range(2):
        waits = [load(pout, pout_v)] if h == 0 else []
        waits.append(load(og.at[rows[h]], og_v.at[at[h]]))
        jobs.append((waits, "r", h, 0, og.shape[1]))
    for h in range(2):
        k0 = 0
        for width in PARTS[h]:
            ks = pl.ds(k0, width * 256)
            waits = [load(pin.at[:, ks], pin_v.at[:, ks])] if h == 0 else []
            waits.append(load(hid.at[rows[h], ks], hid_v.at[at[h], ks]))
            jobs.append((waits, "l", h, k0, width * 256))
            k0 += width * 256
    q_load = load(queries, q_v)

    barrier = pltpu.get_barrier_semaphore()
    for o in FAR:
        pl.semaphore_signal(barrier, inc=1, device_id=peer(o)[4], device_id_type=MESH)
    for d in FAR_Z:
        pl.semaphore_signal(barrier, inc=1, device_id=along_z(d)[1], device_id_type=MESH)

    def project(job):
        waits, side, h, k0, width = job
        for copy in waits:
            copy.wait()

        @pl.when(live)
        def _():
            lo = h * HALF
            if side == "r":
                acc[0, lo : lo + HALF] = lax.dot_general(
                    og_v[lo : lo + HALF], pout_v[...], NT, preferred_element_type=F32
                )
            else:
                term = lax.dot_general(
                    hid_v[lo : lo + HALF, k0 : k0 + width], pin_v[:, k0 : k0 + width], NT, preferred_element_type=F32
                )
                if k0 == 0:
                    acc[1, lo : lo + HALF] = term
                else:
                    acc[1, lo : lo + HALF] += term

    def to_sibling(side):
        sib_out[side] = acc[side, 0:HALF].T
        copy = remote(sib_out.at[side], sib_in.at[side], sib_send.at[side], sib_recv.at[side], peer((0, 0, 1))[4])
        copy.start()
        return copy

    project(jobs[0])
    pl.semaphore_wait(barrier, len(FAR) + len(FAR_Z))
    sib_r = to_sibling(0)
    project(jobs[1])
    project(jobs[2])
    sib_r.wait_recv()
    right[...] = acc[0, HALF:].T + sib_in[0]
    for o in FAR:
        x2, y2, c2, slot, device = peer(o)
        remote(right.at[pl.ds(pl.multiple_of(y2 * 16, 16), 16)], xr.at[me], x_send.at[0], x_recv.at[0], device).start()
    xr[me] = right[pl.ds(pl.multiple_of(y * 16, 16), 16), :]
    first_own = 2 + len(PARTS[0])
    for job in jobs[3:first_own]:
        project(job)
    sib_l = to_sibling(1)
    for job in jobs[first_own:]:
        project(job)
    sib_l.wait_recv()
    left[...] = acc[1, HALF:].T + sib_in[1]
    for o in FAR:
        x2, y2, c2, slot, device = peer(o)
        remote(left.at[pl.ds(pl.multiple_of((2 * x2 + c2) * 8, 8), 8)], xl.at[me], x_send.at[1], x_recv.at[1], device).start()
    xl[me] = left[pl.ds(pl.multiple_of((2 * x + c) * 8, 8), 8), :]

    lane_group = lax.broadcasted_iota(jnp.int32, (16, 128), 1) // 16
    q_load.wait()
    for bi in range(8):
        rolled = []
        for p in range(4):
            block = q_v[:, (bi * 4 + p) * 128 : (bi * 4 + p + 1) * 128]
            rolled.append(block if p == 0 else pltpu.roll(block, 16 * p, 1))
        for bj in range(4):
            pick = (lane_group + (4 - bj)) % 4
            out = rolled[3]
            for p in range(3):
                out = jnp.where(pick == p, rolled[p], out)
            qs[((bi // 2) * Y + bj) * 2 + bi % 2] = out
    for o in FAR:
        slot, device = peer(o)[3:]
        remote(qs.at[slot], qr.at[me], x_send.at[2], x_recv.at[2], device).start()
    qr[me] = qs[me]

    lane = lax.broadcasted_iota(jnp.int32, (8, DOCS), 1)
    lengths = jnp.broadcast_to(lens[...], (8, DOCS))
    ends = lengths
    for shift in (1, 2, 4, 8, 16, 32, 64):
        ends = ends + jnp.where(lane >= shift, pltpu.roll(ends, shift, 1), 0)
    starts = (ends - lengths)[0:1]
    ends = ends[0:1]
    token = lax.broadcasted_iota(jnp.int32, (HALF, DOCS), 0)
    for k in range(PLANE):
        t = token + (((k // 2) * Z + z) * TOK + (k % 2) * HALF)
        inside = (starts <= t) & (t < ends)
        member[k * HALF : (k + 1) * HALF, :] = jnp.where(inside, 1.0, 0.0).astype(BF16)

    settle(xr.at[pl.ds(0, PLANE - 1)], x_recv.at[0])
    settle(xl.at[pl.ds(0, PLANE - 1)], x_recv.at[1])
    groups = [(4 * (i % 2) + y + i // 2) % 8 for i in range(8)]
    for k in range(PLANE):
        r = xr[k]
        l = xl[k]
        for i in range(8):
            hi, lo = split(l[i : i + 1, :] * r)
            outer[0, groups[i], :, k * HALF : (k + 1) * HALF] = hi
            outer[1, groups[i], :, k * HALF : (k + 1) * HALF] = lo
    both = dot(outer[...].reshape(256, PLANE * HALF), member[...])
    part[...] = both[0:128] + both[128:256]

    for d in FAR_Z:
        z2, device = along_z(d)
        remote(part.at[pl.ds(pl.multiple_of(z2 * 16, 16), 16)], rs.at[z], z_send.at[0], z_recv.at[0], device).start()
    rs[z] = part[pl.ds(pl.multiple_of(z * 16, 16), 16), :]
    settle(qr.at[pl.ds(0, PLANE - 1)], x_recv.at[2])
    for k in range(PLANE):
        hi, lo = split(qr[k])
        qcat[16 * k : 16 * k + 16, 0:128] = hi
        qcat[16 * k : 16 * k + 16, 128:256] = lo
    settle(rs.at[pl.ds(0, Z - 1)], z_recv.at[0])
    total = rs[0]
    for k in range(1, Z):
        total = total + rs[k]
    mine[...] = total
    for d in FAR_Z:
        device = along_z(d)[1]
        remote(mine, ag.at[z], z_send.at[1], z_recv.at[1], device).start()
    ag[z] = total
    chip = lax.broadcasted_iota(jnp.int32, (16, DOCS), 0)
    chosen = jnp.where(owner[...] == chip * Z + z, 1.0, 0.0).astype(BF16)
    settle(ag.at[pl.ds(0, Z - 1)], z_recv.at[1])

    grads = ag[...].reshape(128, DOCS)
    hi, lo = split(grads)
    squares = jnp.sum(grads * grads, axis=0, keepdims=True)
    partial_scores = dot(qcat[...], jnp.concatenate([hi, hi], axis=0)) + dot(qcat[:, 0:128], lo)
    row_part = lax.dot_general(chosen, hi, NT, preferred_element_type=F32) + lax.dot_general(
        chosen, lo, NT, preferred_element_type=F32
    )
    which = lax.broadcasted_iota(jnp.int32, (8, 128), 0)
    for k in range(PLANE):
        fs[k, 0:16] = partial_scores[16 * k : 16 * k + 16]
        fs[k, 16:24] = jnp.where(which == 0, squares, jnp.where(which == 1, row_part[k // 2 : k // 2 + 1], 0.0))
    for o in FAR:
        slot, device = peer(o)[3:]
        remote(fs.at[slot], fr.at[me], x_send.at[3], x_recv.at[3], device).start()
    fr[me] = fs[me]
    settle(fr.at[pl.ds(0, PLANE - 1)], x_recv.at[3])

    summed = fr[0]
    for k in range(1, PLANE):
        summed = summed + fr[k]
    inverse = 1.0 / jnp.sqrt(summed[16:17] * (1.0 / COLS) + 1e-06)
    scores[...] = summed[0:16] * inverse
    own = jnp.sum(jnp.where(owner[...] == s, inverse, 0.0), axis=1, keepdims=True)
    lanes = lax.broadcasted_iota(jnp.int32, (8, 128), 1) // 16
    tiles = [
        jnp.concatenate([fr[((bi // 2) * Y + bj) * 2 + bi % 2, 17:18, :] for bi in range(8)], axis=0) * own
        for bj in range(4)
    ]
    for p in range(4):
        pick = (lanes + (4 - p)) % 4
        out = tiles[3]
        for bj in range(3):
            out = jnp.where(pick == bj, tiles[bj], out)
        if p:
            out = pltpu.roll(out, 128 - 16 * p, 1)
        for bi in range(8):
            store[0:1, (bi * 4 + p) * 128 : (bi * 4 + p + 1) * 128] = out[bi : bi + 1]

    sib_r.wait_send()
    sib_l.wait_send()
    settle(xr.at[pl.ds(0, PLANE - 1)], x_send.at[0])
    settle(xl.at[pl.ds(0, PLANE - 1)], x_send.at[1])
    settle(qr.at[pl.ds(0, PLANE - 1)], x_send.at[2])
    settle(fr.at[pl.ds(0, PLANE - 1)], x_send.at[3])
    settle(rs.at[pl.ds(0, Z - 1)], z_send.at[0])
    settle(ag.at[pl.ds(0, Z - 1)], z_send.at[1])


def per_device(hidden_acts, out_grads, proj_in, proj_out, doc_lengths, owner, queries):
    anywhere = pl.BlockSpec(memory_space=pl.ANY)
    vmem = pl.BlockSpec(memory_space=pltpu.VMEM)
    width, model = hidden_acts.shape[1], out_grads.shape[1]
    dma = pltpu.SemaphoreType.DMA
    return pl.pallas_call(
        kernel,
        out_shape=(jax.ShapeDtypeStruct((1, COLS), F32), jax.ShapeDtypeStruct((16, DOCS), F32)),
        in_specs=[anywhere] * 4 + [vmem] * 2 + [anywhere],
        out_specs=(vmem, vmem),
        scratch_shapes=[
            pltpu.VMEM((TOK, width), BF16),
            pltpu.VMEM((TOK, model), BF16),
            pltpu.VMEM((RANK, width), BF16),
            pltpu.VMEM((RANK, model), BF16),
            pltpu.VMEM((16, COLS), F32),
            pltpu.VMEM((2, TOK, RANK), F32),
            pltpu.VMEM((2, RANK, HALF), F32),
            pltpu.VMEM((2, RANK, HALF), F32),
            pltpu.VMEM((RANK, HALF), F32),
            pltpu.VMEM((RANK, HALF), F32),
            pltpu.VMEM((PLANE, 16, HALF), F32),
            pltpu.VMEM((PLANE, 8, HALF), F32),
            pltpu.VMEM((PLANE * HALF, DOCS), BF16),
            pltpu.VMEM((2, 8, 16, PLANE * HALF), BF16),
            pltpu.VMEM((PLANE, 16, 128), F32),
            pltpu.VMEM((PLANE, 16, 128), F32),
            pltpu.VMEM((PLANE * 16, 256), BF16),
            pltpu.VMEM((128, DOCS), F32),
            pltpu.VMEM((Z, 16, DOCS), F32),
            pltpu.VMEM((16, DOCS), F32),
            pltpu.VMEM((Z, 16, DOCS), F32),
            pltpu.VMEM((PLANE, 24, DOCS), F32),
            pltpu.VMEM((PLANE, 24, DOCS), F32),
            dma((16,)),
            dma((2,)),
            dma((2,)),
            dma((4,)),
            dma((4,)),
            dma((2,)),
            dma((2,)),
        ],
        compiler_params=pltpu.CompilerParams(
            collective_id=1, has_side_effects=True, vmem_limit_bytes=56 << 20
        ),
        name="influence",
    )(hidden_acts, out_grads, proj_in.T, proj_out.T, doc_lengths[None], owner[None], queries)


def solution(mesh):
    in_specs = (
        P("seq", "tp"),
        P("seq", "tp"),
        P("tp", None),
        P("tp", None),
        P(),
        P(),
        P(("seq", "tp"), None),
    )
    out_specs = (P("seq", None), P(("seq", "tp"), None))
    return jax.shard_map(per_device, mesh=mesh, in_specs=in_specs, out_specs=out_specs, check_vma=False)
```

time: 312 us -> 42.2 us (0.14)
  waiting for transfers between devices: 279 us -> 0 us
  Pallas kernels: 0 us -> 38.7 us
  between operations: 14.1 us -> 0.64 us
  matrix products: 13.3 us -> 0 us
  other arithmetic: 3.17 us -> 0 us
    psum x1 -> x0, waiting for transfers between devices: 262 us -> none  [per_device(): grads = lax.psum(partial_table, ('seq', 'tp'))]
    pallas_call x0 -> x1, Pallas kernels: none -> 38.7 us  [per_device(): pl.pallas_call(kernel, out_shape=(jax.ShapeDtypeStruct((1, COLS), F32), j...]
    reduce_scatter x1 -> x0, waiting for transfers between devices: 17 us -> none  [per_device(): halves = lax.psum_scatter(stacked, 'tp', scatter_dimension=0, tiled=True)]
    dot_general x5 -> x0, matrix products: 13.3 us -> none  [the longest x1 6.08 us: per_device(): jnp.dot(hidden_acts, proj_in, preferred_element_type=jnp.float32)]
  transfers between devices with their start and end apart: 2 -> 0, of which waited for: 2 -> 0; matrix products, arithmetic and copies ran while one was open for 0% -> 0% of each run, Pallas kernels for 0% -> 0%
where the time goes in v1:
time: 42.2 us; the launch traced here: 42 us
  Pallas kernels  38.7 us (92%)
  local copies, waits for them, and re-layouts  2.62 us (6%)
  between operations  0.64 us (2%)
    pallas_call x1, Pallas kernels, per_device(): pl.pallas_call(kernel, out_shape=(jax.ShapeDtypeStruct((1, COLS), F32), j...  38.7 us
    unnamed x2, local copies, waits for them, and re-layouts  2.62 us

profile of v1, /device:TPU:1, one launch (start us, length us, event | category | flops | bytes accessed | tf_op | source)
XLA Modules:
  0.0 42.0 jit_solution(8909342118295878878)
XLA Ops:
  0.6 38.7 %influence.1 = (f32[1,4096]{1,0:T(1,128)}, f32[16,128]{1,0:T(8,128)}) custom-call(bf16[256,14336]{1,0:T(8,128)(2,1)} %hid.1, bf16[256,4096]{1,0:T(8,128)(2,1)} %og.1, bf16[64,14336]{1,0:T(8,128)(2,1)} %bitcast.4, bf16[64,4096]{1,0:T(8,128)(2,1)} %bitcast.5, s32[1,128]{1,0:T(1,128)} %bitcast.6, s32[1,128]{1,0:T(1,128)} %bitcast.7, f32[16,4096]{1,0:T(8,128)} %queries.1), custom_call_target="tpu_custom_call" | custom-call | tf_op jit(solution)/shard_map/influence/pallas_call | solution.py:269
  39.3 1.3 %copy.11 = f32[1,4096]{1,0:T(1,128)} copy(f32[1,4096]{1,0:T(1,128)} %get-tuple-element.4) | data formatting | bytes 32768
  40.7 1.3 %copy.12 = f32[16,128]{1,0:T(8,128)} copy(f32[16,128]{1,0:T(8,128)} %get-tuple-element.5) | data formatting | bytes 16384

commit v2 on v1

v2 whole, which is shorter than its diff:
```python
import jax
import jax.numpy as jnp
from jax import lax
from jax.experimental import pallas as pl
from jax.experimental.pallas import tpu as pltpu
from jax.sharding import PartitionSpec as P

X, Y, Z = 4, 4, 8
RANK = 64
TOK = 256
HALF = 128
DOCS = 128
COLS = RANK * RANK
CHIPS = X * Y
MESH = pl.DeviceIdType.MESH
NT = (((1,), (1,)), ((), ()))
F32, BF16 = jnp.float32, jnp.bfloat16
PARTS = ((20, 20, 16), (20, 20, 12, 4))
PLAN = (0, 1, 2, 3, 4, "meet", "give right", "give left", 5, "send right", 6, 7, 8)


HOPS = (0, 1, 2, 1)
FAR = sorted(range(1, CHIPS), key=lambda o: -(HOPS[o >> 2] + HOPS[o & 3]))
FAR_Z = (4, 5, 7, 6, 3, 2, 1)


def split(v):
    hi = v.astype(BF16)
    return hi, (v - hi.astype(F32)).astype(BF16)


def dot(a, b):
    return jnp.dot(a, b, preferred_element_type=F32)


def kernel(
    hid, og, pin, pout, lens_in, owner_in, queries, store, scores,
    hid_v, og_v, pin_v, pout_v, lens, owner, q_v, acc, sib_out, sib_in, right, left, xr, xl,
    member, outer, qs, qr, qcat, g_out, g_in, part, rs, mine, ag, ag_sib, fs, fr,
    load_sem, sib_send, sib_recv, x_send, x_recv, z_send, z_recv,
):
    s, c = lax.axis_index("seq"), lax.axis_index("tp")
    z = s & (Z - 1)
    me = s >> 3
    x, y = me >> 2, me & 3
    live = s >= 0
    sibling = (s, 1 - c)

    def peer(o):
        chip = me ^ o
        return chip, ((chip << 3) | z, c)

    def along_z(d):
        return z ^ d, (s ^ d, c)

    def remote(src, dst, send, recv, device):
        copy = pltpu.make_async_remote_copy(
            src_ref=src, dst_ref=dst, send_sem=send, recv_sem=recv, device_id=device, device_id_type=MESH
        )
        copy.start()
        return copy

    def to_sibling(n, src, dst):
        return remote(src, dst, sib_send.at[n], sib_recv.at[n], sibling)

    def settle(ref, sem):
        pltpu.make_async_copy(ref, ref, sem).wait()

    def rows(n, size):
        return pl.ds(pl.multiple_of(n * size, size), size)

    started = []

    def load(src, dst):
        copy = pltpu.make_async_copy(src, dst, load_sem.at[len(started)])
        copy.start()
        started.append(copy)
        return copy

    barrier = pltpu.get_barrier_semaphore()

    def announce():
        for o in FAR:
            pl.semaphore_signal(barrier, inc=1, device_id=peer(o)[1], device_id_type=MESH)
        for d in FAR_Z:
            pl.semaphore_signal(barrier, inc=1, device_id=along_z(d)[1], device_id_type=MESH)
        pl.semaphore_signal(barrier, inc=1, device_id=sibling, device_id_type=MESH)

    announce()
    tokens = [rows(1 - c, HALF), rows(c, HALF)]
    jobs = []
    for h in range(2):
        waits = [load(pout, pout_v)] if h == 0 else []
        waits.append(load(og.at[tokens[h]], og_v.at[pl.ds(h * HALF, HALF)]))
        jobs.append((waits, "r", h, 0, og.shape[1]))
    for h in range(2):
        k0 = 0
        for width in PARTS[h]:
            ks = pl.ds(k0, width * 256)
            waits = [load(pin.at[:, ks], pin_v.at[:, ks])] if h == 0 else []
            waits.append(load(hid.at[tokens[h], ks], hid_v.at[pl.ds(h * HALF, HALF), ks]))
            jobs.append((waits, "l", h, k0, width * 256))
            k0 += width * 256
    last_loads = [load(lens_in, lens), load(owner_in, owner), load(queries, q_v)]

    def project(job):
        waits, side, h, k0, width = job
        for copy in waits:
            copy.wait()

        @pl.when(live)
        def _():
            lo = h * HALF
            if side == "r":
                acc[0, lo : lo + HALF] = lax.dot_general(
                    og_v[lo : lo + HALF], pout_v[...], NT, preferred_element_type=F32
                )
            else:
                term = lax.dot_general(
                    hid_v[lo : lo + HALF, k0 : k0 + width], pin_v[:, k0 : k0 + width], NT, preferred_element_type=F32
                )
                if k0 == 0:
                    acc[1, lo : lo + HALF] = term
                else:
                    acc[1, lo : lo + HALF] += term

    sib_copies = {}

    def give(side):
        sib_out[side] = acc[side, 0:HALF].T
        sib_copies[side] = to_sibling(side, sib_out.at[side], sib_in.at[side])

    def send_right():
        sib_copies[0].wait_recv()
        right[...] = acc[0, HALF:].T + sib_in[0]
        for o in FAR:
            chip, device = peer(o)
            remote(right.at[rows(chip & 3, 16)], xr.at[me], x_send.at[0], x_recv.at[0], device)
        xr[me] = right[rows(y, 16), :]

    for step in PLAN:
        if step == "meet":
            pl.semaphore_wait(barrier, len(FAR) + len(FAR_Z) + 1)
        elif step == "give right":
            give(0)
        elif step == "give left":
            give(1)
        elif step == "send right":
            send_right()
        else:
            project(jobs[step])
    sib_copies[1].wait_recv()
    left[...] = acc[1, HALF:].T + sib_in[1]
    for o in FAR:
        chip, device = peer(o)
        remote(left.at[rows(chip >> 2, 16)], xl.at[me], x_send.at[1], x_recv.at[1], device)
    xl[me] = left[rows(x, 16), :]

    lane_group = lax.broadcasted_iota(jnp.int32, (16, 128), 1) // 16
    for copy in last_loads:
        copy.wait()
    for bi in range(8):
        rolled = []
        for p in range(4):
            block = q_v[:, (bi * 4 + p) * 128 : (bi * 4 + p + 1) * 128]
            rolled.append(block if p == 0 else pltpu.roll(block, 16 * p, 1))
        for bj in range(4):
            pick = (lane_group + (4 - bj)) % 4
            out = rolled[3]
            for p in range(3):
                out = jnp.where(pick == p, rolled[p], out)
            qs[(bi // 2) * Y + bj, bi % 2] = out
    for o in FAR:
        chip, device = peer(o)
        remote(qs.at[chip], qr.at[:, me], x_send.at[2], x_recv.at[2], device)
    for half in range(2):
        qr[half, me] = qs[me, half]

    lane = lax.broadcasted_iota(jnp.int32, (8, DOCS), 1)
    lengths = jnp.broadcast_to(lens[...], (8, DOCS))
    ends = lengths
    for shift in (1, 2, 4, 8, 16, 32, 64):
        ends = ends + jnp.where(lane >= shift, pltpu.roll(ends, shift, 1), 0)
    starts = (ends - lengths)[0:1]
    ends = ends[0:1]
    token = lax.broadcasted_iota(jnp.int32, (HALF, DOCS), 0) + (z * TOK + c * HALF)
    for k in range(CHIPS):
        t = token + k * (Z * TOK)
        inside = (starts <= t) & (t < ends)
        member[k * HALF : (k + 1) * HALF, :] = jnp.where(inside, 1.0, 0.0).astype(BF16)

    settle(xr.at[pl.ds(0, CHIPS - 1)], x_recv.at[0])
    settle(xl.at[pl.ds(0, CHIPS - 1)], x_recv.at[1])
    groups = [(4 * (i % 2) + y + i // 2) & 7 for i in range(8)]

    def sums(half, n):
        for k in range(CHIPS):
            r = xr[k]
            l = xl[k, rows(half, 8), :]
            for i in range(8):
                hi, lo = split(l[i : i + 1, :] * r)
                outer[n, 0, groups[i], :, k * HALF : (k + 1) * HALF] = hi
                outer[n, 1, groups[i], :, k * HALF : (k + 1) * HALF] = lo
        both = dot(outer[n].reshape(256, CHIPS * HALF), member[...])
        return both[0:128] + both[128:256]

    g_out[...] = sums(1 - c, 0)
    g_copy = to_sibling(2, g_out, g_in)
    own_sums = sums(c, 1)
    g_copy.wait_recv()
    part[...] = own_sums + g_in[...]

    for d in FAR_Z:
        z2, device = along_z(d)
        remote(part.at[rows(z2, 16)], rs.at[z], z_send.at[0], z_recv.at[0], device)
    rs[z] = part[rows(z, 16), :]

    settle(qr.at[:, pl.ds(0, CHIPS - 1)], x_recv.at[2])
    for n, half in enumerate((c, 1 - c)):
        for k in range(CHIPS):
            hi, lo = split(qr[half, k])
            qcat[n, 16 * k : 16 * k + 16, 0:128] = hi
            qcat[n, 16 * k : 16 * k + 16, 128:256] = lo
    settle(rs.at[pl.ds(0, Z - 1)], z_recv.at[0])
    total = rs[0]
    for k in range(1, Z):
        total = total + rs[k]
    mine[...] = total
    for d in FAR_Z:
        device = along_z(d)[1]
        remote(mine, ag.at[z], z_send.at[1], z_recv.at[1], device)
    ag[z] = total
    chip_row = lax.broadcasted_iota(jnp.int32, (CHIPS, DOCS), 0)
    chosen = jnp.where(owner[...] == chip_row * Z + z, 1.0, 0.0).astype(BF16)
    settle(ag.at[pl.ds(0, Z - 1)], z_recv.at[1])

    ag_copy = to_sibling(3, ag, ag_sib)

    def score(n, table):
        grads = table[...].reshape(128, DOCS)
        hi, lo = split(grads)
        row_part = lax.dot_general(chosen, hi, NT, preferred_element_type=F32) + lax.dot_general(
            chosen, lo, NT, preferred_element_type=F32
        )
        part_scores = dot(qcat[n], jnp.concatenate([hi, hi], axis=0)) + dot(qcat[n, :, 0:128], lo)
        return part_scores, jnp.sum(grads * grads, axis=0, keepdims=True), row_part

    own_scores, own_squares, own_row = score(0, ag)
    ag_copy.wait_recv()
    sib_scores, sib_squares, sib_row = score(1, ag_sib)
    both_scores = own_scores + sib_scores
    squares = own_squares + sib_squares
    first_core = c == 0
    row_0 = jnp.where(first_core, own_row, sib_row)
    row_1 = jnp.where(first_core, sib_row, own_row)
    for k in range(CHIPS):
        fs[k, 0:16] = both_scores[16 * k : 16 * k + 16]
        fs[k, 16:17] = squares
        fs[k, 17:18] = row_0[k : k + 1]
        fs[k, 18:19] = row_1[k : k + 1]
    for o in FAR:
        chip, device = peer(o)
        remote(fs.at[chip], fr.at[me], x_send.at[3], x_recv.at[3], device)
    fr[me] = fs[me]
    settle(fr.at[pl.ds(0, CHIPS - 1)], x_recv.at[3])

    summed = fr[0]
    for k in range(1, CHIPS):
        summed = summed + fr[k]
    inverse = 1.0 / jnp.sqrt(summed[16:17] * (1.0 / COLS) + 1e-06)
    scores[...] = summed[0:16] * inverse
    own = jnp.sum(jnp.where(owner[...] == s, inverse, 0.0), axis=1, keepdims=True)
    lanes = lax.broadcasted_iota(jnp.int32, (8, 128), 1) // 16
    tiles = [
        jnp.concatenate([fr[(bi // 2) * Y + bj, 17 + bi % 2 : 18 + bi % 2, :] for bi in range(8)], axis=0) * own
        for bj in range(4)
    ]
    for p in range(4):
        pick = (lanes + (4 - p)) % 4
        out = tiles[3]
        for bj in range(3):
            out = jnp.where(pick == bj, tiles[bj], out)
        if p:
            out = pltpu.roll(out, 128 - 16 * p, 1)
        for bi in range(8):
            store[0:1, (bi * 4 + p) * 128 : (bi * 4 + p + 1) * 128] = out[bi : bi + 1]

    for copy in (sib_copies[0], sib_copies[1], g_copy, ag_copy):
        copy.wait_send()
    settle(xr.at[pl.ds(0, CHIPS - 1)], x_send.at[0])
    settle(xl.at[pl.ds(0, CHIPS - 1)], x_send.at[1])
    settle(qr.at[:, pl.ds(0, CHIPS - 1)], x_send.at[2])
    settle(fr.at[pl.ds(0, CHIPS - 1)], x_send.at[3])
    settle(rs.at[pl.ds(0, Z - 1)], z_send.at[0])
    settle(ag.at[pl.ds(0, Z - 1)], z_send.at[1])


def finish(row, partial, store, scores):
    store[...] = row[...]
    scores[...] = partial[...]


def per_device(hidden_acts, out_grads, proj_in, proj_out, doc_lengths, owner, queries):
    anywhere = pl.BlockSpec(memory_space=pl.ANY)
    vmem = pl.BlockSpec(memory_space=pltpu.VMEM)
    width, model = hidden_acts.shape[1], out_grads.shape[1]
    dma = pltpu.SemaphoreType.DMA
    row, partial = pl.pallas_call(
        kernel,
        out_shape=(jax.ShapeDtypeStruct((1, COLS), F32), jax.ShapeDtypeStruct((16, DOCS), F32)),
        in_specs=[anywhere] * 7,
        out_specs=(vmem, vmem),
        scratch_shapes=[
            pltpu.VMEM((TOK, width), BF16),
            pltpu.VMEM((TOK, model), BF16),
            pltpu.VMEM((RANK, width), BF16),
            pltpu.VMEM((RANK, model), BF16),
            pltpu.VMEM((1, DOCS), jnp.int32),
            pltpu.VMEM((1, DOCS), jnp.int32),
            pltpu.VMEM((16, COLS), F32),
            pltpu.VMEM((2, TOK, RANK), F32),
            pltpu.VMEM((2, RANK, HALF), F32),
            pltpu.VMEM((2, RANK, HALF), F32),
            pltpu.VMEM((RANK, HALF), F32),
            pltpu.VMEM((RANK, HALF), F32),
            pltpu.VMEM((CHIPS, 16, HALF), F32),
            pltpu.VMEM((CHIPS, 16, HALF), F32),
            pltpu.VMEM((CHIPS * HALF, DOCS), BF16),
            pltpu.VMEM((2, 2, 8, 16, CHIPS * HALF), BF16),
            pltpu.VMEM((CHIPS, 2, 16, 128), F32),
            pltpu.VMEM((2, CHIPS, 16, 128), F32),
            pltpu.VMEM((2, CHIPS * 16, 256), BF16),
            pltpu.VMEM((128, DOCS), F32),
            pltpu.VMEM((128, DOCS), F32),
            pltpu.VMEM((128, DOCS), F32),
            pltpu.VMEM((Z, 16, DOCS), F32),
            pltpu.VMEM((16, DOCS), F32),
            pltpu.VMEM((Z, 16, DOCS), F32),
            pltpu.VMEM((Z, 16, DOCS), F32),
            pltpu.VMEM((CHIPS, 19, DOCS), F32),
            pltpu.VMEM((CHIPS, 19, DOCS), F32),
            dma((18,)),
            dma((4,)),
            dma((4,)),
            dma((4,)),
            dma((4,)),
            dma((2,)),
            dma((2,)),
        ],
        compiler_params=pltpu.CompilerParams(
            collective_id=1, has_side_effects=True, vmem_limit_bytes=56 << 20
        ),
        name="influence",
    )(hidden_acts, out_grads, proj_in.T, proj_out.T, doc_lengths[None], owner[None], queries)
    return pl.pallas_call(
        finish,
        out_shape=(jax.ShapeDtypeStruct(row.shape, F32), jax.ShapeDtypeStruct(partial.shape, F32)),
        in_specs=[vmem] * 2,
        out_specs=(vmem, vmem),
        name="finish",
    )(row, partial)


def solution(mesh):
    in_specs = (
        P("seq", "tp"),
        P("seq", "tp"),
        P("tp", None),
        P("tp", None),
        P(),
        P(),
        P(("seq", "tp"), None),
    )
    out_specs = (P("seq", None), P(("seq", "tp"), None))
    return jax.shard_map(per_device, mesh=mesh, in_specs=in_specs, out_specs=out_specs, check_vma=False)
```

time: 42.2 us -> 38.2 us (0.905)
  local copies, waits for them, and re-layouts: 2.62 us -> 0 us
  Pallas kernels: 38.7 us -> 37.4 us
    unnamed x2 -> x0, local copies, waits for them, and re-layouts: 2.62 us -> none
    pallas_call x1, Pallas kernels: 38.7 us -> 36.1 us  [per_device(): pl.pallas_call(kernel, out_shape=(jax.ShapeDtypeStruct((1, COLS), F32), j...]
    pallas_call x0 -> x1, Pallas kernels: none -> 1.33 us  [per_device(): pl.pallas_call(finish, out_shape=(jax.ShapeDtypeStruct(row.shape, F32), j...]
where the time goes in v2:
time: 38.2 us; the launch traced here: 38 us
  Pallas kernels  37.4 us (98%)
  between operations  0.64 us (2%)
    pallas_call x1, Pallas kernels, per_device(): pl.pallas_call(kernel, out_shape=(jax.ShapeDtypeStruct((1, COLS), F32), j...  36.1 us
    pallas_call x1, Pallas kernels, per_device(): pl.pallas_call(finish, out_shape=(jax.ShapeDtypeStruct(row.shape, F32), j...  1.33 us

profile of v2, /device:TPU:1, one launch (start us, length us, event | category | flops | bytes accessed | tf_op | source)
XLA Modules:
  0.0 38.0 jit_solution(8570260831550014420)
XLA Ops:
  0.6 36.1 %influence.1 = (f32[1,4096]{1,0:T(1,128)}, f32[16,128]{1,0:T(8,128)}) custom-call(bf16[256,14336]{1,0:T(8,128)(2,1)} %hid.1, bf16[256,4096]{1,0:T(8,128)(2,1)} %og.1, bf16[64,14336]{1,0:T(8,128)(2,1)} %bitcast.4, bf16[64,4096]{1,0:T(8,128)(2,1)} %bitcast.5, s32[1,128]{1,0:T(1,128)} %bitcast.6, s32[1,128]{1,0:T(1,128)} %bitcast.7, f32[16,4096]{1,0:T(8,128)} %queries.1), custom_call_target="tpu_custom_call" | custom-call | tf_op jit(solution)/shard_map/influence/pallas_call | solution.py:308
  36.7 1.3 %finish.1 = (f32[1,4096]{1,0:T(1,128)}, f32[16,128]{1,0:T(8,128)}) custom-call(f32[1,4096]{1,0:T(1,128)} %get-tuple-element.4.row, f32[16,128]{1,0:T(8,128)} %get-tuple-element.5.partial), custom_call_target="tpu_custom_call" | custom-call | tf_op jit(solution)/shard_map/finish/pallas_call | solution.py:355

commit v3 on v2

--- a/solution.py
+++ b/solution.py
@@ -86,7 +86,6 @@
             pl.semaphore_signal(barrier, inc=1, device_id=along_z(d)[1], device_id_type=MESH)
         pl.semaphore_signal(barrier, inc=1, device_id=sibling, device_id_type=MESH)
 
-    announce()
     tokens = [rows(1 - c, HALF), rows(c, HALF)]
     jobs = []
     for h in range(2):
@@ -101,6 +100,8 @@
             waits.append(load(hid.at[tokens[h], ks], hid_v.at[pl.ds(h * HALF, HALF), ks]))
             jobs.append((waits, "l", h, k0, width * 256))
             k0 += width * 256
+            if len(jobs) == 3:
+                announce()
     last_loads = [load(lens_in, lens), load(owner_in, owner), load(queries, q_v)]
 
     def project(job):
@@ -348,15 +349,21 @@
             dma((2,)),
         ],
         compiler_params=pltpu.CompilerParams(
-            collective_id=1, has_side_effects=True, vmem_limit_bytes=56 << 20
+            collective_id=1, has_side_effects=True, vmem_limit_bytes=40 << 20
         ),
         name="influence",
-    )(hidden_acts, out_grads, proj_in.T, proj_out.T, doc_lengths[None], owner[None], queries)
+    )(
+        *[
+            pltpu.with_memory_space_constraint(v, pltpu.HBM)
+            for v in (hidden_acts, out_grads, proj_in.T, proj_out.T, doc_lengths[None], owner[None], queries)
+        ]
+    )
     return pl.pallas_call(
         finish,
         out_shape=(jax.ShapeDtypeStruct(row.shape, F32), jax.ShapeDtypeStruct(partial.shape, F32)),
         in_specs=[vmem] * 2,
         out_specs=(vmem, vmem),
+        compiler_params=pltpu.CompilerParams(vmem_limit_bytes=1 << 20),
         name="finish",
     )(row, partial)
 

time: 38.2 us -> 36.8 us (0.963)
  Pallas kernels: 37.4 us -> 36.1 us
    pallas_call x1, Pallas kernels: 1.33 us -> 0.61 us  [per_device(): pl.pallas_call(finish, out_shape=(jax.ShapeDtypeStruct(row.shape, F32), j...]
    pallas_call x1, Pallas kernels: 36.1 us -> 35.5 us  [per_device(): pl.pallas_call(kernel, out_shape=(jax.ShapeDtypeStruct((1, COLS), F32), j...]
where the time goes in v3:
time: 36.8 us; the launch traced here: 36.7 us
  Pallas kernels  36.1 us (98%)
  between operations  0.64 us (2%)
    pallas_call x1, Pallas kernels, per_device(): pl.pallas_call(kernel, out_shape=(jax.ShapeDtypeStruct((1, COLS), F32), j...  35.5 us

profile of v3, /device:TPU:1, one launch (start us, length us, event | category | flops | bytes accessed | tf_op | source)
XLA Modules:
  0.0 36.7 jit_solution(8524378417858982746)
XLA Ops:
  0.6 35.5 %influence.1 = (f32[1,4096]{1,0:T(1,128)S(1)}, f32[16,128]{1,0:T(8,128)S(1)}) custom-call(bf16[256,14336]{1,0:T(8,128)(2,1)} %hid.1, bf16[256,4096]{1,0:T(8,128)(2,1)} %og.1, bf16[64,14336]{1,0:T(8,128)(2,1)} %bitcast.4, bf16[64,4096]{1,0:T(8,128)(2,1)} %bitcast.5, s32[1,128]{1,0:T(1,128)} %bitcast.6, s32[1,128]{1,0:T(1,128)} %bitcast.7, f32[16,4096]{1,0:T(8,128)} %queries.1), custom_call_target="tpu_custom_call" | custom-call | tf_op jit(solution)/shard_map/influence/pallas_call | solution.py:309
  36.1 0.6 %finish.1 = (f32[1,4096]{1,0:T(1,128)}, f32[16,128]{1,0:T(8,128)}) custom-call(f32[1,4096]{1,0:T(1,128)S(1)} %get-tuple-element.4.row, f32[16,128]{1,0:T(8,128)S(1)} %get-tuple-element.5.partial), custom_call_target="tpu_custom_call" | custom-call | tf_op jit(solution)/shard_map/finish/pallas_call | solution.py:361

commit v4 on v3

--- a/solution.py
+++ b/solution.py
@@ -37,7 +37,8 @@
     hid, og, pin, pout, lens_in, owner_in, queries, store, scores,
     hid_v, og_v, pin_v, pout_v, lens, owner, q_v, acc, sib_out, sib_in, right, left, xr, xl,
     member, outer, qs, qr, qcat, g_out, g_in, part, rs, mine, ag, ag_sib, fs, fr,
-    load_sem, sib_send, sib_recv, x_send, x_recv, z_send, z_recv,
+    q_first, qcat_first, f_first, fr_first,
+    load_sem, sib_send, sib_recv, x_send, x_recv, z_send, z_recv, first_send, first_recv,
 ):
     s, c = lax.axis_index("seq"), lax.axis_index("tp")
     z = s & (Z - 1)
@@ -45,10 +46,14 @@
     x, y = me >> 2, me & 3
     live = s >= 0
     sibling = (s, 1 - c)
+    first = me == 0
 
     def peer(o):
         chip = me ^ o
         return chip, ((chip << 3) | z, c)
+
+    def across(chip):
+        return (chip << 3) | z, 1 - c
 
     def along_z(d):
         return z ^ d, (s ^ d, c)
@@ -85,6 +90,15 @@
         for d in FAR_Z:
             pl.semaphore_signal(barrier, inc=1, device_id=along_z(d)[1], device_id_type=MESH)
         pl.semaphore_signal(barrier, inc=1, device_id=sibling, device_id_type=MESH)
+
+        @pl.when(first)
+        def _():
+            for chip in range(1, CHIPS):
+                pl.semaphore_signal(barrier, inc=1, device_id=across(chip), device_id_type=MESH)
+
+        @pl.when(jnp.logical_not(first))
+        def _():
+            pl.semaphore_signal(barrier, inc=1, device_id=across(0), device_id_type=MESH)
 
     tokens = [rows(1 - c, HALF), rows(c, HALF)]
     jobs = []
@@ -141,7 +155,7 @@
 
     for step in PLAN:
         if step == "meet":
-            pl.semaphore_wait(barrier, len(FAR) + len(FAR_Z) + 1)
+            pl.semaphore_wait(barrier, len(FAR) + len(FAR_Z) + 1 + jnp.where(first, CHIPS - 1, 1))
         elif step == "give right":
             give(0)
         elif step == "give left":
@@ -177,6 +191,11 @@
     for half in range(2):
         qr[half, me] = qs[me, half]
 
+    @pl.when(first)
+    def _():
+        for chip in range(CHIPS):
+            remote(qs.at[chip, 1 - c], q_first, first_send.at[0], first_recv.at[0], across(chip))
+
     lane = lax.broadcasted_iota(jnp.int32, (8, DOCS), 1)
     lengths = jnp.broadcast_to(lens[...], (8, DOCS))
     ends = lengths
@@ -222,6 +241,11 @@
             hi, lo = split(qr[half, k])
             qcat[n, 16 * k : 16 * k + 16, 0:128] = hi
             qcat[n, 16 * k : 16 * k + 16, 128:256] = lo
+    settle(q_first, first_recv.at[0])
+    for n, rows_in in enumerate((qr[c, 0], q_first[...])):
+        hi, lo = split(rows_in)
+        qcat_first[16 * n : 16 * n + 16, 0:128] = hi
+        qcat_first[16 * n : 16 * n + 16, 128:256] = lo
     settle(rs.at[pl.ds(0, Z - 1)], z_recv.at[0])
     total = rs[0]
     for k in range(1, Z):
@@ -240,11 +264,30 @@
     def score(n, table):
         grads = table[...].reshape(128, DOCS)
         hi, lo = split(grads)
+        twice = jnp.concatenate([hi, hi], axis=0)
         row_part = lax.dot_general(chosen, hi, NT, preferred_element_type=F32) + lax.dot_general(
             chosen, lo, NT, preferred_element_type=F32
         )
-        part_scores = dot(qcat[n], jnp.concatenate([hi, hi], axis=0)) + dot(qcat[n, :, 0:128], lo)
-        return part_scores, jnp.sum(grads * grads, axis=0, keepdims=True), row_part
+        squares = jnp.sum(grads * grads, axis=0, keepdims=True)
+        if n == 0:
+            early = dot(qcat_first[...], twice) + dot(qcat_first[:, 0:128], lo)
+            for k in range(2):
+                f_first[k, 0:16] = early[16 * k : 16 * k + 16]
+                f_first[k, 16:17] = squares
+                f_first[k, 17:18] = row_part[0:1]
+            slot = me * 2 + c
+
+            @pl.when(first)
+            def _():
+                fr_first[slot] = f_first[0]
+
+            @pl.when(jnp.logical_not(first))
+            def _():
+                remote(f_first.at[0], fr_first.at[slot], first_send.at[1], first_recv.at[1], (z, c))
+
+            remote(f_first.at[1], fr_first.at[slot], first_send.at[2], first_recv.at[1], (z, 1 - c))
+        part_scores = dot(qcat[n], twice) + dot(qcat[n, :, 0:128], lo)
+        return part_scores, squares, row_part
 
     own_scores, own_squares, own_row = score(0, ag)
     ag_copy.wait_recv()
@@ -261,37 +304,54 @@
         fs[k, 18:19] = row_1[k : k + 1]
     for o in FAR:
         chip, device = peer(o)
-        remote(fs.at[chip], fr.at[me], x_send.at[3], x_recv.at[3], device)
-    fr[me] = fs[me]
-    settle(fr.at[pl.ds(0, CHIPS - 1)], x_recv.at[3])
-
-    summed = fr[0]
-    for k in range(1, CHIPS):
-        summed = summed + fr[k]
-    inverse = 1.0 / jnp.sqrt(summed[16:17] * (1.0 / COLS) + 1e-06)
-    scores[...] = summed[0:16] * inverse
-    own = jnp.sum(jnp.where(owner[...] == s, inverse, 0.0), axis=1, keepdims=True)
-    lanes = lax.broadcasted_iota(jnp.int32, (8, 128), 1) // 16
-    tiles = [
-        jnp.concatenate([fr[(bi // 2) * Y + bj, 17 + bi % 2 : 18 + bi % 2, :] for bi in range(8)], axis=0) * own
-        for bj in range(4)
-    ]
-    for p in range(4):
-        pick = (lanes + (4 - p)) % 4
-        out = tiles[3]
-        for bj in range(3):
-            out = jnp.where(pick == bj, tiles[bj], out)
-        if p:
-            out = pltpu.roll(out, 128 - 16 * p, 1)
-        for bi in range(8):
-            store[0:1, (bi * 4 + p) * 128 : (bi * 4 + p + 1) * 128] = out[bi : bi + 1]
-
+
+        @pl.when(me != o)
+        def _():
+            remote(fs.at[chip], fr.at[me], x_send.at[3], x_recv.at[3], device)
+
+    def results(parts, row):
+        summed = parts(0)
+        for k in range(1, row[0]):
+            summed = summed + parts(k)
+        inverse = 1.0 / jnp.sqrt(summed[16:17] * (1.0 / COLS) + 1e-06)
+        scores[...] = summed[0:16] * inverse
+        own = jnp.sum(jnp.where(owner[...] == s, inverse, 0.0), axis=1, keepdims=True)
+        lanes = lax.broadcasted_iota(jnp.int32, (8, 128), 1) // 16
+        tiles = [
+            jnp.concatenate([row[1]((bi // 2) * Y + bj, bi % 2) for bi in range(8)], axis=0) * own
+            for bj in range(4)
+        ]
+        for p in range(4):
+            pick = (lanes + (4 - p)) % 4
+            out = tiles[3]
+            for bj in range(3):
+                out = jnp.where(pick == bj, tiles[bj], out)
+            if p:
+                out = pltpu.roll(out, 128 - 16 * p, 1)
+            for bi in range(8):
+                store[0:1, (bi * 4 + p) * 128 : (bi * 4 + p + 1) * 128] = out[bi : bi + 1]
+
+    @pl.when(first)
+    def _():
+        settle(fr_first.at[pl.ds(0, 2 * CHIPS - 1)], first_recv.at[1])
+        results(lambda k: fr_first[k], (2 * CHIPS, lambda chip, half: fr_first[2 * chip + half, 17:18, :]))
+        settle(fr.at[pl.ds(0, CHIPS - 1)], x_send.at[3])
+        settle(qs.at[:, 0], first_send.at[0])
+
+    @pl.when(jnp.logical_not(first))
+    def _():
+        fr[me] = fs[me]
+        settle(fr.at[pl.ds(0, CHIPS - 1)], x_recv.at[3])
+        results(lambda k: fr[k], (CHIPS, lambda chip, half: fr[chip, 17 + half : 18 + half, :]))
+        settle(fr.at[pl.ds(0, CHIPS - 2)], x_send.at[3])
+        settle(f_first.at[0], first_send.at[1])
+
+    settle(f_first.at[1], first_send.at[2])
     for copy in (sib_copies[0], sib_copies[1], g_copy, ag_copy):
         copy.wait_send()
     settle(xr.at[pl.ds(0, CHIPS - 1)], x_send.at[0])
     settle(xl.at[pl.ds(0, CHIPS - 1)], x_send.at[1])
     settle(qr.at[:, pl.ds(0, CHIPS - 1)], x_send.at[2])
-    settle(fr.at[pl.ds(0, CHIPS - 1)], x_send.at[3])
     settle(rs.at[pl.ds(0, Z - 1)], z_send.at[0])
     settle(ag.at[pl.ds(0, Z - 1)], z_send.at[1])
 
@@ -340,12 +400,18 @@
             pltpu.VMEM((Z, 16, DOCS), F32),
             pltpu.VMEM((CHIPS, 19, DOCS), F32),
             pltpu.VMEM((CHIPS, 19, DOCS), F32),
+            pltpu.VMEM((16, 128), F32),
+            pltpu.VMEM((32, 256), BF16),
+            pltpu.VMEM((2, 18, DOCS), F32),
+            pltpu.VMEM((2 * CHIPS, 18, DOCS), F32),
             dma((18,)),
             dma((4,)),
             dma((4,)),
             dma((4,)),
             dma((4,)),
             dma((2,)),
+            dma((2,)),
+            dma((3,)),
             dma((2,)),
         ],
         compiler_params=pltpu.CompilerParams(

time: 36.8 us -> 35.8 us (0.973)
  Pallas kernels: 36.1 us -> 35.1 us
    pallas_call x1, Pallas kernels: 35.5 us -> 34.5 us  [per_device(): pl.pallas_call(kernel, out_shape=(jax.ShapeDtypeStruct((1, COLS), F32), j...]
where the time goes in v4:
time: 35.8 us; the launch traced here: 35.7 us
  Pallas kernels  35.1 us (98%)
  between operations  0.64 us (2%)
    pallas_call x1, Pallas kernels, per_device(): pl.pallas_call(kernel, out_shape=(jax.ShapeDtypeStruct((1, COLS), F32), j...  34.5 us

profile of v4, /device:TPU:1, one launch (start us, length us, event | category | flops | bytes accessed | tf_op | source)
XLA Modules:
  0.0 35.7 jit_solution(1217130419055080949)
XLA Ops:
  0.6 34.5 %influence.1 = (f32[1,4096]{1,0:T(1,128)S(1)}, f32[16,128]{1,0:T(8,128)S(1)}) custom-call(bf16[256,14336]{1,0:T(8,128)(2,1)} %hid.1, bf16[256,4096]{1,0:T(8,128)(2,1)} %og.1, bf16[64,14336]{1,0:T(8,128)(2,1)} %bitcast.4, bf16[64,4096]{1,0:T(8,128)(2,1)} %bitcast.5, s32[1,128]{1,0:T(1,128)} %bitcast.6, s32[1,128]{1,0:T(1,128)} %bitcast.7, f32[16,4096]{1,0:T(8,128)} %queries.1), custom_call_target="tpu_custom_call" | custom-call | tf_op jit(solution)/shard_map/influence/pallas_call | solution.py:369
  35.1 0.6 %finish.1 = (f32[1,4096]{1,0:T(1,128)}, f32[16,128]{1,0:T(8,128)}) custom-call(f32[1,4096]{1,0:T(1,128)S(1)} %get-tuple-element.4.row, f32[16,128]{1,0:T(8,128)S(1)} %get-tuple-element.5.partial), custom_call_target="tpu_custom_call" | custom-call | tf_op jit(solution)/shard_map/finish/pallas_call | solution.py:427

commit v5 on v4

--- a/solution.py
+++ b/solution.py
@@ -15,8 +15,8 @@
 MESH = pl.DeviceIdType.MESH
 NT = (((1,), (1,)), ((), ()))
 F32, BF16 = jnp.float32, jnp.bfloat16
-PARTS = ((20, 20, 16), (20, 20, 12, 4))
-PLAN = (0, 1, 2, 3, 4, "meet", "give right", "give left", 5, "send right", 6, 7, 8)
+PARTS = ((20, 20, 16), (24, 24, 8))
+PLAN = (0, 1, 2, 3, 4, "meet", "give right", "give left", 5, "send right", 6, 7)
 
 
 HOPS = (0, 1, 2, 1)
@@ -76,11 +76,12 @@
 
     started = []
 
-    def load(src, dst):
-        copy = pltpu.make_async_copy(src, dst, load_sem.at[len(started)])
-        copy.start()
-        started.append(copy)
-        return copy
+    def load(*pairs):
+        sem = load_sem.at[len(started)]
+        for src, dst in pairs:
+            pltpu.make_async_copy(src, dst, sem).start()
+        started.append(sem)
+        return sem
 
     barrier = pltpu.get_barrier_semaphore()
 
@@ -103,25 +104,26 @@
     tokens = [rows(1 - c, HALF), rows(c, HALF)]
     jobs = []
     for h in range(2):
-        waits = [load(pout, pout_v)] if h == 0 else []
-        waits.append(load(og.at[tokens[h]], og_v.at[pl.ds(h * HALF, HALF)]))
-        jobs.append((waits, "r", h, 0, og.shape[1]))
+        tail = ((og.at[tokens[h]], og_v.at[pl.ds(h * HALF, HALF)]),)
+        head = ((pout, pout_v),) if h == 0 else ()
+        arrived = og_v.at[pl.ds(0, HALF + RANK * len(head))]
+        jobs.append((load(*head, *tail), arrived, "r", h, 0, og.shape[1]))
     for h in range(2):
         k0 = 0
         for width in PARTS[h]:
             ks = pl.ds(k0, width * 256)
-            waits = [load(pin.at[:, ks], pin_v.at[:, ks])] if h == 0 else []
-            waits.append(load(hid.at[tokens[h], ks], hid_v.at[pl.ds(h * HALF, HALF), ks]))
-            jobs.append((waits, "l", h, k0, width * 256))
+            tail = ((hid.at[tokens[h], ks], hid_v.at[pl.ds(h * HALF, HALF), ks]),)
+            head = ((pin.at[:, ks], pin_v.at[:, ks]),) if h == 0 else ()
+            arrived = hid_v.at[pl.ds(0, HALF + RANK * len(head)), ks]
+            jobs.append((load(*head, *tail), arrived, "l", h, k0, width * 256))
             k0 += width * 256
             if len(jobs) == 3:
                 announce()
-    last_loads = [load(lens_in, lens), load(owner_in, owner), load(queries, q_v)]
+    last_loads = [(load((a, b)), b) for a, b in ((lens_in, lens), (owner_in, owner), (queries, q_v))]
 
     def project(job):
-        waits, side, h, k0, width = job
-        for copy in waits:
-            copy.wait()
+        sem, arrived, side, h, k0, width = job
+        settle(arrived, sem)
 
         @pl.when(live)
         def _():
@@ -172,8 +174,8 @@
     xl[me] = left[rows(x, 16), :]
 
     lane_group = lax.broadcasted_iota(jnp.int32, (16, 128), 1) // 16
-    for copy in last_loads:
-        copy.wait()
+    for sem, ref in last_loads:
+        settle(ref, sem)
     for bi in range(8):
         rolled = []
         for p in range(4):
@@ -331,22 +333,6 @@
             for bi in range(8):
                 store[0:1, (bi * 4 + p) * 128 : (bi * 4 + p + 1) * 128] = out[bi : bi + 1]
 
-    @pl.when(first)
-    def _():
-        settle(fr_first.at[pl.ds(0, 2 * CHIPS - 1)], first_recv.at[1])
-        results(lambda k: fr_first[k], (2 * CHIPS, lambda chip, half: fr_first[2 * chip + half, 17:18, :]))
-        settle(fr.at[pl.ds(0, CHIPS - 1)], x_send.at[3])
-        settle(qs.at[:, 0], first_send.at[0])
-
-    @pl.when(jnp.logical_not(first))
-    def _():
-        fr[me] = fs[me]
-        settle(fr.at[pl.ds(0, CHIPS - 1)], x_recv.at[3])
-        results(lambda k: fr[k], (CHIPS, lambda chip, half: fr[chip, 17 + half : 18 + half, :]))
-        settle(fr.at[pl.ds(0, CHIPS - 2)], x_send.at[3])
-        settle(f_first.at[0], first_send.at[1])
-
-    settle(f_first.at[1], first_send.at[2])
     for copy in (sib_copies[0], sib_copies[1], g_copy, ag_copy):
         copy.wait_send()
     settle(xr.at[pl.ds(0, CHIPS - 1)], x_send.at[0])
@@ -354,6 +340,22 @@
     settle(qr.at[:, pl.ds(0, CHIPS - 1)], x_send.at[2])
     settle(rs.at[pl.ds(0, Z - 1)], z_send.at[0])
     settle(ag.at[pl.ds(0, Z - 1)], z_send.at[1])
+    settle(f_first.at[1], first_send.at[2])
+
+    @pl.when(first)
+    def _():
+        settle(qs.at[:, 0], first_send.at[0])
+        settle(fr.at[pl.ds(0, CHIPS - 1)], x_send.at[3])
+        settle(fr_first.at[pl.ds(0, 2 * CHIPS - 1)], first_recv.at[1])
+        results(lambda k: fr_first[k], (2 * CHIPS, lambda chip, half: fr_first[2 * chip + half, 17:18, :]))
+
+    @pl.when(jnp.logical_not(first))
+    def _():
+        fr[me] = fs[me]
+        settle(f_first.at[0], first_send.at[1])
+        settle(fr.at[pl.ds(0, CHIPS - 2)], x_send.at[3])
+        settle(fr.at[pl.ds(0, CHIPS - 1)], x_recv.at[3])
+        results(lambda k: fr[k], (CHIPS, lambda chip, half: fr[chip, 17 + half : 18 + half, :]))
 
 
 def finish(row, partial, store, scores):

time: 35.8 us -> 35.8 us (level)
  no operation moved by 1% of the time
where the time goes in v5:
time: 35.8 us
  Pallas kernels  35.1 us (98%)
  between operations  0.64 us (2%)
    pallas_call x1, Pallas kernels, per_device(): pl.pallas_call(kernel, out_shape=(jax.ShapeDtypeStruct((1, COLS), F32), j...  34.5 us

profile of v5, /device:TPU:1, one launch (start us, length us, event | category | flops | bytes accessed | tf_op | source)
XLA Modules:
  0.0 35.8 jit_solution(3241077521954108459)
XLA Ops:
  0.6 34.5 %influence.1 = (f32[1,4096]{1,0:T(1,128)S(1)}, f32[16,128]{1,0:T(8,128)S(1)}) custom-call(bf16[256,14336]{1,0:T(8,128)(2,1)} %hid.1, bf16[256,4096]{1,0:T(8,128)(2,1)} %og.1, bf16[64,14336]{1,0:T(8,128)(2,1)} %bitcast.4, bf16[64,4096]{1,0:T(8,128)(2,1)} %bitcast.5, s32[1,128]{1,0:T(1,128)} %bitcast.6, s32[1,128]{1,0:T(1,128)} %bitcast.7, f32[16,4096]{1,0:T(8,128)} %queries.1), custom_call_target="tpu_custom_call" | custom-call | tf_op jit(solution)/shard_map/influence/pallas_call | solution.py:371
  35.1 0.6 %finish.1 = (f32[1,4096]{1,0:T(1,128)}, f32[16,128]{1,0:T(8,128)}) custom-call(f32[1,4096]{1,0:T(1,128)S(1)} %get-tuple-element.4.row, f32[16,128]{1,0:T(8,128)S(1)} %get-tuple-element.5.partial), custom_call_target="tpu_custom_call" | custom-call | tf_op jit(solution)/shard_map/finish/pallas_call | solution.py:429

commit v6 on v5

--- a/solution.py
+++ b/solution.py
@@ -21,7 +21,7 @@
 
 HOPS = (0, 1, 2, 1)
 FAR = sorted(range(1, CHIPS), key=lambda o: -(HOPS[o >> 2] + HOPS[o & 3]))
-FAR_Z = (4, 5, 7, 6, 3, 2, 1)
+FAR_Z = (4, 3, 5, 2, 6, 7, 1)
 
 
 def split(v):
@@ -46,14 +46,12 @@
     x, y = me >> 2, me & 3
     live = s >= 0
     sibling = (s, 1 - c)
-    first = me == 0
+    first = (me == 0) & (c == 1)
+    to_first = (z, 1)
 
     def peer(o):
         chip = me ^ o
         return chip, ((chip << 3) | z, c)
-
-    def across(chip):
-        return (chip << 3) | z, 1 - c
 
     def along_z(d):
         return z ^ d, (s ^ d, c)
@@ -95,11 +93,11 @@
         @pl.when(first)
         def _():
             for chip in range(1, CHIPS):
-                pl.semaphore_signal(barrier, inc=1, device_id=across(chip), device_id_type=MESH)
-
-        @pl.when(jnp.logical_not(first))
-        def _():
-            pl.semaphore_signal(barrier, inc=1, device_id=across(0), device_id_type=MESH)
+                pl.semaphore_signal(barrier, inc=1, device_id=((chip << 3) | z, 0), device_id_type=MESH)
+
+        @pl.when((c == 0) & (me != 0))
+        def _():
+            pl.semaphore_signal(barrier, inc=1, device_id=to_first, device_id_type=MESH)
 
     tokens = [rows(1 - c, HALF), rows(c, HALF)]
     jobs = []
@@ -157,7 +155,7 @@
 
     for step in PLAN:
         if step == "meet":
-            pl.semaphore_wait(barrier, len(FAR) + len(FAR_Z) + 1 + jnp.where(first, CHIPS - 1, 1))
+            pl.semaphore_wait(barrier, len(FAR) + len(FAR_Z) + 1 + jnp.where(first, CHIPS - 1, jnp.where((c == 0) & (me != 0), 1, 0)))
         elif step == "give right":
             give(0)
         elif step == "give left":
@@ -196,7 +194,7 @@
     @pl.when(first)
     def _():
         for chip in range(CHIPS):
-            remote(qs.at[chip, 1 - c], q_first, first_send.at[0], first_recv.at[0], across(chip))
+            remote(qs.at[chip, 0], q_first, first_send.at[0], first_recv.at[0], ((chip << 3) | z, 0))
 
     lane = lax.broadcasted_iota(jnp.int32, (8, DOCS), 1)
     lengths = jnp.broadcast_to(lens[...], (8, DOCS))
@@ -243,11 +241,18 @@
             hi, lo = split(qr[half, k])
             qcat[n, 16 * k : 16 * k + 16, 0:128] = hi
             qcat[n, 16 * k : 16 * k + 16, 128:256] = lo
-    settle(q_first, first_recv.at[0])
-    for n, rows_in in enumerate((qr[c, 0], q_first[...])):
-        hi, lo = split(rows_in)
-        qcat_first[16 * n : 16 * n + 16, 0:128] = hi
-        qcat_first[16 * n : 16 * n + 16, 128:256] = lo
+
+    @pl.when(c == 0)
+    def _():
+        settle(q_first, first_recv.at[0])
+
+    @pl.when(c == 1)
+    def _():
+        q_first[...] = qr[1, 0]
+
+    hi, lo = split(q_first[...])
+    qcat_first[:, 0:128] = hi
+    qcat_first[:, 128:256] = lo
     settle(rs.at[pl.ds(0, Z - 1)], z_recv.at[0])
     total = rs[0]
     for k in range(1, Z):
@@ -273,21 +278,19 @@
         squares = jnp.sum(grads * grads, axis=0, keepdims=True)
         if n == 0:
             early = dot(qcat_first[...], twice) + dot(qcat_first[:, 0:128], lo)
-            for k in range(2):
-                f_first[k, 0:16] = early[16 * k : 16 * k + 16]
-                f_first[k, 16:17] = squares
-                f_first[k, 17:18] = row_part[0:1]
+            f_first[0:16] = early
+            f_first[16:17] = squares
+            f_first[17:18] = row_part[0:1]
             slot = me * 2 + c
 
             @pl.when(first)
             def _():
-                fr_first[slot] = f_first[0]
+                fr_first[slot] = f_first[...]
 
             @pl.when(jnp.logical_not(first))
             def _():
-                remote(f_first.at[0], fr_first.at[slot], first_send.at[1], first_recv.at[1], (z, c))
-
-            remote(f_first.at[1], fr_first.at[slot], first_send.at[2], first_recv.at[1], (z, 1 - c))
+                remote(f_first, fr_first.at[slot], first_send.at[1], first_recv.at[1], to_first)
+
         part_scores = dot(qcat[n], twice) + dot(qcat[n, :, 0:128], lo)
         return part_scores, squares, row_part
 
@@ -307,7 +310,7 @@
     for o in FAR:
         chip, device = peer(o)
 
-        @pl.when(me != o)
+        @pl.when((c == 0) | (me != o))
         def _():
             remote(fs.at[chip], fr.at[me], x_send.at[3], x_recv.at[3], device)
 
@@ -340,7 +343,6 @@
     settle(qr.at[:, pl.ds(0, CHIPS - 1)], x_send.at[2])
     settle(rs.at[pl.ds(0, Z - 1)], z_send.at[0])
     settle(ag.at[pl.ds(0, Z - 1)], z_send.at[1])
-    settle(f_first.at[1], first_send.at[2])
 
     @pl.when(first)
     def _():
@@ -352,8 +354,16 @@
     @pl.when(jnp.logical_not(first))
     def _():
         fr[me] = fs[me]
-        settle(f_first.at[0], first_send.at[1])
-        settle(fr.at[pl.ds(0, CHIPS - 2)], x_send.at[3])
+        settle(f_first, first_send.at[1])
+
+        @pl.when(c == 0)
+        def _():
+            settle(fr.at[pl.ds(0, CHIPS - 1)], x_send.at[3])
+
+        @pl.when(c == 1)
+        def _():
+            settle(fr.at[pl.ds(0, CHIPS - 2)], x_send.at[3])
+
         settle(fr.at[pl.ds(0, CHIPS - 1)], x_recv.at[3])
         results(lambda k: fr[k], (CHIPS, lambda chip, half: fr[chip, 17 + half : 18 + half, :]))
 
@@ -403,8 +413,8 @@
             pltpu.VMEM((CHIPS, 19, DOCS), F32),
             pltpu.VMEM((CHIPS, 19, DOCS), F32),
             pltpu.VMEM((16, 128), F32),
-            pltpu.VMEM((32, 256), BF16),
-            pltpu.VMEM((2, 18, DOCS), F32),
+            pltpu.VMEM((16, 256), BF16),
+            pltpu.VMEM((18, DOCS), F32),
             pltpu.VMEM((2 * CHIPS, 18, DOCS), F32),
             dma((18,)),
             dma((4,)),
@@ -413,7 +423,7 @@
             dma((4,)),
             dma((2,)),
             dma((2,)),
-            dma((3,)),
+            dma((2,)),
             dma((2,)),
         ],
         compiler_params=pltpu.CompilerParams(

time: 35.8 us -> 35.7 us (level)
  no operation moved by 1% of the time
where the time goes in v6:
time: 35.7 us
  Pallas kernels  35 us (98%)
  between operations  0.64 us (2%)
    pallas_call x1, Pallas kernels, per_device(): pl.pallas_call(kernel, out_shape=(jax.ShapeDtypeStruct((1, COLS), F32), j...  34.4 us

profile of v6, /device:TPU:1, one launch (start us, length us, event | category | flops | bytes accessed | tf_op | source)
XLA Modules:
  0.0 35.7 jit_solution(16900102473445133514)
XLA Ops:
  0.6 34.4 %influence.1 = (f32[1,4096]{1,0:T(1,128)S(1)}, f32[16,128]{1,0:T(8,128)S(1)}) custom-call(bf16[256,14336]{1,0:T(8,128)(2,1)} %hid.1, bf16[256,4096]{1,0:T(8,128)(2,1)} %og.1, bf16[64,14336]{1,0:T(8,128)(2,1)} %bitcast.4, bf16[64,4096]{1,0:T(8,128)(2,1)} %bitcast.5, s32[1,128]{1,0:T(1,128)} %bitcast.6, s32[1,128]{1,0:T(1,128)} %bitcast.7, f32[16,4096]{1,0:T(8,128)} %queries.1), custom_call_target="tpu_custom_call" | custom-call | tf_op jit(solution)/shard_map/influence/pallas_call | solution.py:381
  35.0 0.6 %finish.1 = (f32[1,4096]{1,0:T(1,128)}, f32[16,128]{1,0:T(8,128)}) custom-call(f32[1,4096]{1,0:T(1,128)S(1)} %get-tuple-element.4.row, f32[16,128]{1,0:T(8,128)S(1)} %get-tuple-element.5.partial), custom_call_target="tpu_custom_call" | custom-call | tf_op jit(solution)/shard_map/finish/pallas_call | solution.py:439

commit v7 on v5

--- a/solution.py
+++ b/solution.py
@@ -187,17 +187,6 @@
             for p in range(3):
                 out = jnp.where(pick == p, rolled[p], out)
             qs[(bi // 2) * Y + bj, bi % 2] = out
-    for o in FAR:
-        chip, device = peer(o)
-        remote(qs.at[chip], qr.at[:, me], x_send.at[2], x_recv.at[2], device)
-    for half in range(2):
-        qr[half, me] = qs[me, half]
-
-    @pl.when(first)
-    def _():
-        for chip in range(CHIPS):
-            remote(qs.at[chip, 1 - c], q_first, first_send.at[0], first_recv.at[0], across(chip))
-
     lane = lax.broadcasted_iota(jnp.int32, (8, DOCS), 1)
     lengths = jnp.broadcast_to(lens[...], (8, DOCS))
     ends = lengths
@@ -237,6 +226,28 @@
         remote(part.at[rows(z2, 16)], rs.at[z], z_send.at[0], z_recv.at[0], device)
     rs[z] = part[rows(z, 16), :]
 
+    for o in FAR:
+        chip, device = peer(o)
+        remote(qs.at[chip], qr.at[:, me], x_send.at[2], x_recv.at[2], device)
+    for half in range(2):
+        qr[half, me] = qs[me, half]
+
+    @pl.when(first)
+    def _():
+        for chip in range(CHIPS):
+            remote(qs.at[chip, 1 - c], q_first, first_send.at[0], first_recv.at[0], across(chip))
+
+    settle(rs.at[pl.ds(0, Z - 1)], z_recv.at[0])
+    total = rs[0]
+    for k in range(1, Z):
+        total = total + rs[k]
+    mine[...] = total
+    for d in FAR_Z:
+        device = along_z(d)[1]
+        remote(mine, ag.at[z], z_send.at[1], z_recv.at[1], device)
+    ag[z] = total
+    chip_row = lax.broadcasted_iota(jnp.int32, (CHIPS, DOCS), 0)
+    chosen = jnp.where(owner[...] == chip_row * Z + z, 1.0, 0.0).astype(BF16)
     settle(qr.at[:, pl.ds(0, CHIPS - 1)], x_recv.at[2])
     for n, half in enumerate((c, 1 - c)):
         for k in range(CHIPS):
@@ -248,17 +259,6 @@
         hi, lo = split(rows_in)
         qcat_first[16 * n : 16 * n + 16, 0:128] = hi
         qcat_first[16 * n : 16 * n + 16, 128:256] = lo
-    settle(rs.at[pl.ds(0, Z - 1)], z_recv.at[0])
-    total = rs[0]
-    for k in range(1, Z):
-        total = total + rs[k]
-    mine[...] = total
-    for d in FAR_Z:
-        device = along_z(d)[1]
-        remote(mine, ag.at[z], z_send.at[1], z_recv.at[1], device)
-    ag[z] = total
-    chip_row = lax.broadcasted_iota(jnp.int32, (CHIPS, DOCS), 0)
-    chosen = jnp.where(owner[...] == chip_row * Z + z, 1.0, 0.0).astype(BF16)
     settle(ag.at[pl.ds(0, Z - 1)], z_recv.at[1])
 
     ag_copy = to_sibling(3, ag, ag_sib)

time: 35.8 us -> 35.8 us (level)
  no operation moved by 1% of the time
where the time goes in v7:
time: 35.8 us; the launch traced here: 35.7 us
  Pallas kernels  35.1 us (98%)
  between operations  0.64 us (2%)
    pallas_call x1, Pallas kernels, per_device(): pl.pallas_call(kernel, out_shape=(jax.ShapeDtypeStruct((1, COLS), F32), j...  34.4 us

profile of v7, /device:TPU:1, one launch (start us, length us, event | category | flops | bytes accessed | tf_op | source)
XLA Modules:
  0.0 35.7 jit_solution(2519505527682475691)
XLA Ops:
  0.6 34.4 %influence.1 = (f32[1,4096]{1,0:T(1,128)S(1)}, f32[16,128]{1,0:T(8,128)S(1)}) custom-call(bf16[256,14336]{1,0:T(8,128)(2,1)} %hid.1, bf16[256,4096]{1,0:T(8,128)(2,1)} %og.1, bf16[64,14336]{1,0:T(8,128)(2,1)} %bitcast.4, bf16[64,4096]{1,0:T(8,128)(2,1)} %bitcast.5, s32[1,128]{1,0:T(1,128)} %bitcast.6, s32[1,128]{1,0:T(1,128)} %bitcast.7, f32[16,4096]{1,0:T(8,128)} %queries.1), custom_call_target="tpu_custom_call" | custom-call | tf_op jit(solution)/shard_map/influence/pallas_call | solution.py:371
  35.1 0.6 %finish.1 = (f32[1,4096]{1,0:T(1,128)}, f32[16,128]{1,0:T(8,128)}) custom-call(f32[1,4096]{1,0:T(1,128)S(1)} %get-tuple-element.4.row, f32[16,128]{1,0:T(8,128)S(1)} %get-tuple-element.5.partial), custom_call_target="tpu_custom_call" | custom-call | tf_op jit(solution)/shard_map/finish/pallas_call | solution.py:429
